TPU v7x, 512 devices: a whole 4x8x8 slice. The times are simulated.
512 devices in a mesh: dp: 32 (over x, z), tensor: 16 (over y, core).
Axes of the slice: x: 4, y: 8, z: 8, core: 2. Of those that a mesh axis runs over, the one named last changes fastest.
Arguments:
- policy_logits: bfloat16 [4096, 77824], P('dp', 'tensor'), may hold values from -50 to 250
- reference_logits: bfloat16 [4096, 77824], P('dp', 'tensor'), may hold values from -50 to 250
- targets: int32 [4096], P('dp'), may hold values from 0 to 77823
- loss_mask: int32 [4096], P('dp'), may hold values 0 or 1
- partner: int32 [256], P('dp'), may hold values from 0 to 255, as said below
- chosen: int32 [256], P('dp'), may hold values from 0 to 1, as said below
Outputs:
- logit_grad: float32 [4096, 77824], P('dp', 'tensor')
- pair_loss: float32 [256], P('dp')
Inputs may be any that keep to these rules, and one draw needn't show every extreme that they name: partner[partner[s]] = s and partner[s] != s for every sequence s. Exactly one sequence of each pair has chosen = 1.
All inputs are finite; a program needn't handle non-finite values. No bound on the sum of `loss_mask` on one device may be relied on, other than what follows from the above.
Results may differ from a plain program's by a relative error of at most 0.0003.
Values may be sent and summed in bfloat16 or wider, within the bound.
A program may use at most 64 MiB of HBM per device.

v0:
```python
import jax
import jax.numpy as jnp
from jax import lax
from jax.sharding import PartitionSpec as P

beta_scale = 0.5
kl_scale = 0.25


def pair_terms(seq_table, own_stats, partner, chosen):
    seq_count = seq_table.shape[0]
    matches = partner[:, None] == jnp.arange(seq_count, dtype=jnp.int32)[None, :]
    partner_stats = jnp.sum(jnp.where(matches[:, :, None], seq_table[None, :, :], 0.0), axis=1)
    chosen_f = chosen.astype(jnp.float32)
    sign_value = 2.0 * chosen_f - 1.0
    margin = sign_value * (
        beta_scale * (own_stats[:, 0] - partner_stats[:, 0])
        + kl_scale * (own_stats[:, 1] - partner_stats[:, 1])
    )
    slope_value = -jax.nn.sigmoid(-margin)
    return (
        jax.nn.softplus(-margin),
        beta_scale * sign_value * slope_value,
        -kl_scale * (1.0 - chosen_f) * slope_value,
    )


def finish_rows(row_set):
    peak_policy, total_policy, peak_refer, total_refer, cross_sum, pick_policy, pick_refer = row_set
    norm_policy = peak_policy + jnp.log(total_policy)
    norm_refer = peak_refer + jnp.log(total_refer)
    kl_row = cross_sum / total_refer - norm_refer + norm_policy
    ratio_row = pick_policy - norm_policy - (pick_refer - norm_refer)
    return (norm_policy, norm_refer, kl_row, ratio_row)


def row_grad(
    policy_vals, refer_vals, target_hits, norm_policy, norm_refer, mask_rows, coef_ratio, coef_kl
):
    prob_policy = jnp.exp(policy_vals - norm_policy[:, None])
    prob_refer = jnp.exp(refer_vals - norm_refer[:, None])
    onehot = target_hits.astype(jnp.float32)
    return mask_rows[:, None] * (
        coef_ratio[:, None] * (onehot - prob_policy) + coef_kl[:, None] * (prob_policy - prob_refer)
    )


def shards(policy_logits, reference_logits, targets, loss_mask, partner, chosen):
    rows_dev, vocab_width = policy_logits.shape
    seqs_dev = partner.shape[0]
    seq_length = rows_dev // seqs_dev
    mask_all = loss_mask.astype(jnp.float32)
    vocab_start = lax.axis_index("tensor") * vocab_width
    policy_vals = policy_logits.astype(jnp.float32)
    refer_vals = reference_logits.astype(jnp.float32)
    columns = vocab_start + jnp.arange(vocab_width, dtype=jnp.int32)
    target_hits = columns[None, :] == targets[:, None]
    peak_policy, peak_refer = lax.pmax(
        (jnp.max(policy_vals, axis=1), jnp.max(refer_vals, axis=1)), "tensor"
    )
    expo_refer = jnp.exp(refer_vals - peak_refer[:, None])
    total_policy, total_refer, cross_sum, pick_policy, pick_refer = lax.psum(
        (
            jnp.sum(jnp.exp(policy_vals - peak_policy[:, None]), axis=1),
            jnp.sum(expo_refer, axis=1),
            jnp.sum(expo_refer * (refer_vals - policy_vals), axis=1),
            jnp.sum(jnp.where(target_hits, policy_vals, 0.0), axis=1),
            jnp.sum(jnp.where(target_hits, refer_vals, 0.0), axis=1),
        ),
        "tensor",
    )
    row_set = (
        peak_policy,
        total_policy,
        peak_refer,
        total_refer,
        cross_sum,
        pick_policy,
        pick_refer,
    )
    norm_policy, norm_refer, kl_row, ratio_row = finish_rows(row_set)
    seq_ratio = jnp.sum((mask_all * ratio_row).reshape(seqs_dev, seq_length), axis=1)
    seq_kl = jnp.sum((mask_all * kl_row).reshape(seqs_dev, seq_length), axis=1)
    own_stats = jnp.stack([seq_ratio, seq_kl], axis=1)
    seq_table = lax.all_gather(own_stats, "dp", axis=0, tiled=True)
    pair_loss, coef_ratio, coef_kl = pair_terms(seq_table, own_stats, partner, chosen)
    ratio_rows = jnp.repeat(coef_ratio, seq_length, total_repeat_length=rows_dev)
    kl_rows = jnp.repeat(coef_kl, seq_length, total_repeat_length=rows_dev)
    logit_grad = row_grad(
        policy_vals, refer_vals, target_hits, norm_policy, norm_refer, mask_all, ratio_rows, kl_rows
    )
    return (logit_grad, pair_loss)


def solution(mesh):
    return jax.shard_map(
        shards,
        mesh=mesh,
        in_specs=(P("dp", "tensor"), P("dp", "tensor"), P("dp"), P("dp"), P("dp"), P("dp")),
        out_specs=(P("dp", "tensor"), P("dp")),
        check_vma=False,
    )
```

profile of v0, /device:TPU:6, one launch (start us, length us, event | category | flops | bytes accessed | tf_op | source)
XLA Modules:
  0.0 120.5 jit_solution(14049435955216716334)
XLA Ops:
  0.6 0.0 copy-start.10
  0.6 0.0 copy-start.1
  0.7 0.0 copy-start.11
  0.7 0.0 copy-start.3
  0.7 0.0 copy-start.4
  0.7 0.0 copy-start.5
  0.7 0.0 copy-start.6
  0.7 0.0 copy-start.7
  0.8 0.0 copy-start.8
  0.8 0.0 copy-start.9
  0.8 1.7 %reduce_max.28 = bf16[128]{0:T(256)(128)(2,1)S(1)} reduce(bf16[128,4864]{1,0:T(8,128)(2,1)} %param.12, bf16[]{:T(256)} %constant.107.clone.1), dimensions={1}, to_apply=%region_2.0 | reduce | flops 622464 | bytes 1245442 | tf_op jit(solution)/shard_map/reduce_max | solution.py:59
  2.5 1.5 %reduce_max.30 = bf16[128]{0:T(256)(128)(2,1)S(1)} reduce(bf16[128,4864]{1,0:T(8,128)(2,1)} %param.13, bf16[]{:T(256)} %constant.107.clone.1), dimensions={1}, to_apply=%region_8.9 | reduce | flops 622464 | bytes 1245442 | tf_op jit(solution)/shard_map/reduce_max | solution.py:59
  4.0 26.9 %all-reduce.1 = (f32[128]{0:T(128)S(1)}, f32[128]{0:T(128)S(1)}) all-reduce(bf16[128]{0:T(256)(128)(2,1)S(1)} %reduce_max.30, bf16[128]{0:T(256)(128)(2,1)S(1)} %reduce_max.28), channel_id=1, replica_groups=mesh['dp'=32,'tensor'=16] {'tensor'}, use_global_device_ids=true, to_apply=%region_9.10 | all-reduce | flops 256 | bytes 1536 | tf_op jit(solution)/shard_map/pmax | solution.py:58
  30.9 0.0 copy-done.10
  31.0 0.1 iota_compare_fusion
  31.1 0.0 copy-done.1
  31.1 1.8 %fusion.4 = (f32[128]{0:T(128)S(1)}, f32[128]{0:T(128)S(1)}, f32[128]{0:T(128)S(1)}, f32[128]{0:T(128)S(1)}, f32[128]{0:T(128)S(1)}) fusion(bf16[128,4864]{1,0:T(8,128)(2,1)S(1)} %copy-done, s32[4864]{0:T(1024)S(1)} %iota_add_fusion, s32[128]{0:T(128)S(1)} %copy-done.2, f32[128]{0:T(128)S(1)} %get-tuple-element.36, f32[128]{0:T(128)S(1)} %get-tuple-element.35, ...), kind=kLoop, calls=%fused_computation.12 | loop fusion | flops 8715648 | bytes 2513920 | tf_op jit(solution)/shard_map/reduce_sum | solution.py:67
  32.8 23.5 %all-reduce = (f32[128]{0:T(128)S(1)}, f32[128]{0:T(128)S(1)}, f32[128]{0:T(128)S(1)}, f32[128]{0:T(128)S(1)}, f32[128]{0:T(128)S(1)}) all-reduce(f32[128]{0:T(128)S(1)} %get-tuple-element.27, f32[128]{0:T(128)S(1)} %get-tuple-element.26, f32[128]{0:T(128)S(1)} %get-tuple-element.28, ...), channel_id=1, replica_groups=mesh['dp'=32,'tensor'=16] {'tensor'}, use_global_device_ids=true, to_apply=%region_11.12 | all-reduce | flops 640 | bytes 5120 | tf_op jit(solution)/shard_map/psum | solution.py:62
  56.4 0.1 reshape.93
  56.5 0.1 reduce_sum.76
  56.6 0.1 reshape.94
  56.7 0.1 reduce_sum.78
  56.8 48.6 %all-gather = f32[32,8,2]{1,2,0:T(2,128)S(1)} all-gather(f32[1,8,2]{1,2,0:T(2,128)S(1)} %maximum_bitcast_fusion), channel_id=1, replica_groups=mesh['dp'=32,'tensor'=16] {'dp'}, dimensions={0}, use_global_device_ids=true | all-gather | bytes 2112 | tf_op jit(solution)/shard_map/all_gather | solution.py:85
  105.5 0.1 reshape.126
  105.6 0.1 select_reduce_fusion
  105.6 0.0 copy-done.11
  105.6 0.5 compare_select_fusion
  106.2 0.7 fusion.22
  106.9 4.9 %select_select_fusion = f32[128]{0:T(128)S(1)} fusion(pred[128]{0:T(512)(128)(4,1)S(1)} %copy-done.9, pred[128]{0:T(512)(128)(4,1)S(1)} %copy-done.8, pred[128]{0:T(512)(128)(4,1)S(1)} %copy-done.7, pred[128]{0:T(512)(128)(4,1)S(1)} %copy-done.6, pred[128]{0:T(512)(128)(4,1)S(1)} %copy-done.5, pred[128]{0:T(512)(128)(4,1)S(1)} %copy-done.4, ...), kind=kLoop, calls=%fused_computation.35 | loop fusion | flops 896 | bytes 1440 | tf_op jit(solution)/shard_map/jit(_take)/gather | solution.py:88
  111.9 0.7 fusion.21
  112.6 4.9 %select_select_fusion.1 = f32[128]{0:T(128)S(1)} fusion(pred[128]{0:T(512)(128)(4,1)S(1)} %copy-done.9, pred[128]{0:T(512)(128)(4,1)S(1)} %copy-done.8, pred[128]{0:T(512)(128)(4,1)S(1)} %copy-done.7, pred[128]{0:T(512)(128)(4,1)S(1)} %copy-done.6, pred[128]{0:T(512)(128)(4,1)S(1)} %copy-done.5, pred[128]{0:T(512)(128)(4,1)S(1)} %copy-done.4, ...), kind=kLoop, calls=%fused_computation.36 | loop fusion | flops 896 | bytes 1440 | tf_op jit(solution)/shard_map/jit(_take)/gather | solution.py:87
  117.5 3.0 %fusion.3 = f32[128,4864]{1,0:T(8,128)} fusion(bf16[128,4864]{1,0:T(8,128)(2,1)S(1)} %copy-done, bf16[128,4864]{1,0:T(8,128)(2,1)S(1)} %copy-done.1, f32[128]{0:T(128)S(1)} %get-tuple-element.43, f32[128]{0:T(128)S(1)} %select_select_fusion, f32[128]{0:T(128)S(1)} %get-tuple-element.42, f32[128]{0:T(128)S(1)} %select_select_fusion.1, ...), kind=kLoop, calls=%fused_computation.11 | loop fusion | flops 7471104 | bytes 5003264 | tf_op jit(solution)/shard_map/mul | solution.py:43
  (21 shorter events, 0.1 us)
Async XLA Ops:
  0.6 30.3 %copy-start.10 = (s32[128]{0:T(128)S(1)}, s32[128]{0:T(128)}, u32[]{:S(2)}) copy-start(s32[128]{0:T(128)} %param.15) | copy-start | bytes 1540
  0.6 30.4 %copy-start.1 = (bf16[128,4864]{1,0:T(8,128)(2,1)S(1)}, bf16[128,4864]{1,0:T(8,128)(2,1)}, u32[]{:S(2)}) copy-start(bf16[128,4864]{1,0:T(8,128)(2,1)} %param.13) | copy-start | bytes 3735556
  0.7 30.4 %copy-start = (bf16[128,4864]{1,0:T(8,128)(2,1)S(1)}, bf16[128,4864]{1,0:T(8,128)(2,1)}, u32[]{:S(2)}) copy-start(bf16[128,4864]{1,0:T(8,128)(2,1)} %param.12) | copy-start | bytes 3735556
  0.7 30.4 %copy-start.2 = (s32[128]{0:T(128)S(1)}, s32[128]{0:T(128)}, u32[]{:S(2)}) copy-start(s32[128]{0:T(128)} %param.14) | copy-start | bytes 1540
  0.7 30.3 %copy-start.12 = (s32[8]{0:T(128)S(1)}, s32[8]{0:T(128)}, u32[]{:S(2)}) copy-start(s32[8]{0:T(128)} %param.16) | copy-start | bytes 100
  0.7 105.0 %copy-start.11 = (s32[8]{0:T(128)S(1)}, s32[8]{0:T(128)}, u32[]{:S(2)}) copy-start(s32[8]{0:T(128)} %param.17) | copy-start | bytes 100
  0.7 106.2 %copy-start.3 = (pred[128]{0:T(512)(128)(4,1)S(1)}, pred[128]{0:T(512)(128)(4,1)}, u32[]{:S(2)}) copy-start(pred[128]{0:T(512)(128)(4,1)} %constant.155) | copy-start | bytes 388
  0.7 106.2 %copy-start.4 = (pred[128]{0:T(512)(128)(4,1)S(1)}, pred[128]{0:T(512)(128)(4,1)}, u32[]{:S(2)}) copy-start(pred[128]{0:T(512)(128)(4,1)} %constant.154) | copy-start | bytes 388
  0.7 106.2 %copy-start.5 = (pred[128]{0:T(512)(128)(4,1)S(1)}, pred[128]{0:T(512)(128)(4,1)}, u32[]{:S(2)}) copy-start(pred[128]{0:T(512)(128)(4,1)} %constant.153) | copy-start | bytes 388
  0.7 106.2 %copy-start.6 = (pred[128]{0:T(512)(128)(4,1)S(1)}, pred[128]{0:T(512)(128)(4,1)}, u32[]{:S(2)}) copy-start(pred[128]{0:T(512)(128)(4,1)} %constant.152) | copy-start | bytes 388
  0.7 106.2 %copy-start.7 = (pred[128]{0:T(512)(128)(4,1)S(1)}, pred[128]{0:T(512)(128)(4,1)}, u32[]{:S(2)}) copy-start(pred[128]{0:T(512)(128)(4,1)} %constant.151) | copy-start | bytes 388
  0.8 106.2 %copy-start.8 = (pred[128]{0:T(512)(128)(4,1)S(1)}, pred[128]{0:T(512)(128)(4,1)}, u32[]{:S(2)}) copy-start(pred[128]{0:T(512)(128)(4,1)} %constant.150) | copy-start | bytes 388
  0.8 106.2 %copy-start.9 = (pred[128]{0:T(512)(128)(4,1)S(1)}, pred[128]{0:T(512)(128)(4,1)}, u32[]{:S(2)}) copy-start(pred[128]{0:T(512)(128)(4,1)} %constant.149) | copy-start | bytes 388
where the time goes:
time: 121 us; the launch traced here: 120 us
  blocking collectives  99.1 us (82%)
  other arithmetic  18.8 us (16%)
  local copies, waits for them, and re-layouts  1.67 us (1%)
    all_gather x1, blocking collectives, shards(): seq_table = lax.all_gather(own_stats, 'dp', axis=0, tiled=True)  48.6 us
    pmax x1, blocking collectives, shards(): lax.pmax((jnp.max(policy_vals, axis=1), jnp.max(refer_vals, axis=1)), 'te...  26.9 us
    psum x1, blocking collectives, shards(): lax.psum((jnp.sum(jnp.exp(policy_vals - peak_policy[:, None]), axis=1), j...  23.5 us
    gather x1, other arithmetic, shards(): jnp.repeat(coef_ratio, seq_length, total_repeat_length=rows_dev)  4.95 us
    gather x1, other arithmetic, shards(): kl_rows = jnp.repeat(coef_kl, seq_length, total_repeat_length=rows_dev)  4.95 us
    mul x1, other arithmetic, row_grad(): mask_rows[:, None]  2.95 us

commit v1 on v0

v1 whole, which is shorter than its diff:
```python
import functools
import jax
import jax.numpy as jnp
from jax import lax
from jax.experimental import pallas as pl
from jax.experimental.pallas import tpu as pltpu
from jax.sharding import PartitionSpec as P

beta_scale = 0.5
kl_scale = 0.25
MESH = pl.DeviceIdType.MESH
LANES = 128
CHUNK = 16
TINY = -3.0e38


def stats_kernel(
    n_dp,
    n_tensor,
    p_hbm,
    r_hbm,
    targets_hbm,
    mask_hbm,
    partner_hbm,
    chosen_hbm,
    grad_ref,
    slope_ref,
    loss_ref,
    p_buf,
    r_buf,
    ep_buf,
    er_buf,
    rows_int,
    ids,
    lane_stats,
    column_set,
    own_rows,
    all_rows,
    own_seqs,
    all_seqs,
    chunk_sems,
    small_sems,
    row_send,
    row_recv,
    seq_send,
    seq_recv,
):
    rows, width = p_buf.shape
    tiles = width // LANES
    chunks = rows // CHUNK
    seqs = partner_hbm.shape[0]
    length = rows // seqs
    my_dp = lax.axis_index("dp")
    my_tensor = lax.axis_index("tensor")

    small = [
        pltpu.make_async_copy(targets_hbm, rows_int.at[0], small_sems.at[0]),
        pltpu.make_async_copy(mask_hbm, rows_int.at[1], small_sems.at[1]),
        pltpu.make_async_copy(partner_hbm, ids.at[0], small_sems.at[2]),
        pltpu.make_async_copy(chosen_hbm, ids.at[1], small_sems.at[3]),
    ]
    for copy in small:
        copy.start()

    def chunk_copies(c):
        here = pl.ds(pl.multiple_of(c * CHUNK, CHUNK), CHUNK)
        return (
            pltpu.make_async_copy(p_hbm.at[here], p_buf.at[here], chunk_sems.at[0, c]),
            pltpu.make_async_copy(r_hbm.at[here], r_buf.at[here], chunk_sems.at[1, c]),
        )

    for c in range(chunks):
        for copy in chunk_copies(c):
            copy.start()

    barrier = pltpu.get_barrier_semaphore()
    for k in range(1, n_tensor):
        pl.semaphore_signal(
            barrier,
            inc=1,
            device_id={"tensor": lax.rem(my_tensor + k, n_tensor)},
            device_id_type=MESH,
        )
    for k in range(1, n_dp):
        pl.semaphore_signal(
            barrier, inc=1, device_id={"dp": lax.rem(my_dp + k, n_dp)}, device_id_type=MESH
        )

    for copy in small:
        copy.wait()
    targets_row = rows_int[0:1, :] - my_tensor * width
    mask_row = rows_int[1:2, :].astype(jnp.float32)
    sub_r = lax.broadcasted_iota(jnp.int32, (LANES, LANES), 0)
    lane_r = lax.broadcasted_iota(jnp.int32, (LANES, LANES), 1)
    stacked = jnp.where(
        sub_r == 0, targets_row.astype(jnp.float32), jnp.where(sub_r == 1, mask_row, 0.0)
    )
    columns = stacked.T
    column_set[0] = (
        jnp.broadcast_to(columns[:, 0:1], (LANES, LANES)).astype(jnp.int32) - lane_r
    )
    mask_col = jnp.broadcast_to(columns[:, 1:2], (LANES, LANES))

    def one_chunk(c, carry):
        for copy in chunk_copies(c):
            copy.wait()
        here = pl.ds(pl.multiple_of(c * CHUNK, CHUNK), CHUNK)
        top_p = p_buf[here, pl.ds(0, LANES)]
        top_r = r_buf[here, pl.ds(0, LANES)]
        for t in range(1, tiles):
            top_p = jnp.maximum(top_p, p_buf[here, pl.ds(t * LANES, LANES)])
            top_r = jnp.maximum(top_r, r_buf[here, pl.ds(t * LANES, LANES)])
        top_p = top_p.astype(jnp.float32)
        top_r = top_r.astype(jnp.float32)
        hits = column_set[0, here, :]
        sum_p = jnp.zeros((CHUNK, LANES), jnp.float32)
        sum_r = sum_p
        cross = sum_p
        pick = sum_p
        for t in range(tiles):
            cols = pl.ds(t * LANES, LANES)
            p = p_buf[here, cols].astype(jnp.float32)
            r = r_buf[here, cols].astype(jnp.float32)
            e_p = jnp.exp(p - top_p)
            e_r = jnp.exp(r - top_r)
            gap = r - p
            ep_buf[here, cols] = e_p
            er_buf[here, cols] = e_r
            sum_p += e_p
            sum_r += e_r
            cross += e_r * gap
            pick += jnp.where(hits == t * LANES, gap, 0.0)
        lane_stats[0, here, :] = top_p
        lane_stats[1, here, :] = top_r
        lane_stats[2, here, :] = sum_p
        lane_stats[3, here, :] = sum_r
        lane_stats[4, here, :] = cross
        lane_stats[5, here, :] = pick
        return carry

    lax.fori_loop(0, chunks, one_chunk, 0)

    top_p = lane_stats[0]
    top_r = lane_stats[1]
    peak_p = jnp.max(top_p, axis=1, keepdims=True)
    peak_r = jnp.max(top_r, axis=1, keepdims=True)
    scale_p = jnp.exp(top_p - peak_p)
    scale_r = jnp.exp(top_r - peak_r)
    total_p = jnp.sum(lane_stats[2] * scale_p, axis=1, keepdims=True)
    total_r = jnp.sum(lane_stats[3] * scale_r, axis=1, keepdims=True)
    cross = jnp.sum(lane_stats[4] * scale_r, axis=1, keepdims=True)
    pick = jnp.sum(lane_stats[5], axis=1, keepdims=True)
    part_p = peak_p + jnp.log(total_p)
    part_r = peak_r + jnp.log(total_r)
    packed = jnp.where(
        lane_r == 0,
        part_p,
        jnp.where(
            lane_r == 1,
            part_r,
            jnp.where(lane_r == 2, cross / total_r, jnp.where(lane_r == 3, pick, 0.0)),
        ),
    )
    own = packed.T[0:8, :]
    own_rows[...] = own
    all_rows[my_tensor] = own

    pl.semaphore_wait(barrier, n_tensor + n_dp - 2)
    for k in range(1, n_tensor):
        pltpu.make_async_remote_copy(
            src_ref=own_rows,
            dst_ref=all_rows.at[my_tensor],
            send_sem=row_send,
            recv_sem=row_recv,
            device_id={"tensor": lax.rem(my_tensor + k, n_tensor)},
            device_id_type=MESH,
        ).start()

    sub_s = lax.broadcasted_iota(jnp.int32, (seqs, LANES), 0)
    lane_s = lax.broadcasted_iota(jnp.int32, (seqs, LANES), 1)
    partner_col = jnp.zeros((seqs, LANES), jnp.int32)
    chosen_col = jnp.zeros((seqs, LANES), jnp.float32)
    for j in range(seqs):
        partner_col = jnp.where(sub_s == j, ids[0, j], partner_col)
        chosen_col = jnp.where(sub_s == j, ids[1, j].astype(jnp.float32), chosen_col)
    sign_col = 2.0 * chosen_col - 1.0
    block_s = lane_s // length == sub_s

    others = all_rows.at[pl.ds(0, n_tensor - 1)]
    pltpu.make_async_copy(others, others, row_recv).wait()
    parts = [all_rows[k] for k in range(n_tensor)]
    peak = functools.reduce(jnp.maximum, parts)
    weights = [jnp.exp(part - peak) for part in parts]
    total = functools.reduce(jnp.add, weights)
    norm = peak + jnp.log(total)
    cross_row = functools.reduce(
        jnp.add, [w[1:2, :] * part[2:3, :] for w, part in zip(weights, parts)]
    )
    pick_row = functools.reduce(jnp.add, parts)[3:4, :]
    norm_p = norm[0:1, :]
    norm_r = norm[1:2, :]
    kl_row = cross_row / total[1:2, :] - norm_r + norm_p
    ratio_row = norm_r - norm_p - pick_row
    value_row = mask_row * (beta_scale * ratio_row + kl_scale * kl_row)
    own_col = jnp.sum(jnp.where(block_s, value_row, 0.0), axis=1, keepdims=True)
    own = jnp.sum(jnp.where(block_s, own_col, 0.0), axis=0, keepdims=True)
    own_seqs[...] = own
    all_seqs[pl.ds(my_dp, 1), :] = own

    for k in range(1, n_dp):
        pltpu.make_async_remote_copy(
            src_ref=own_seqs,
            dst_ref=all_seqs.at[pl.ds(my_dp, 1)],
            send_sem=seq_send,
            recv_sem=seq_recv,
            device_id={"dp": lax.rem(my_dp + k, n_dp)},
            device_id_type=MESH,
        ).start()

    stacked = jnp.where(sub_r == 0, norm_p, jnp.where(sub_r == 1, norm_r, 0.0))
    columns = stacked.T
    chosen_rows = jnp.concatenate(
        [jnp.broadcast_to(chosen_col[j : j + 1, :], (length, LANES)) for j in range(seqs)], axis=0
    )
    coef_hit = mask_col * (beta_scale * (2.0 * chosen_rows - 1.0))
    coef_kl = mask_col * (-kl_scale * (1.0 - chosen_rows))
    column_set[1] = coef_hit.astype(jnp.int32)
    lane_stats[2] = (coef_kl - coef_hit) * jnp.exp(lane_stats[0] - columns[:, 0:1])
    lane_stats[3] = coef_kl * jnp.exp(lane_stats[1] - columns[:, 1:2])
    lane_stats[4] = coef_hit

    def grad_chunk(c, carry):
        here = pl.ds(pl.multiple_of(c * CHUNK, CHUNK), CHUNK)
        hits = column_set[0, here, :]
        scale_p = lane_stats[2, here, :]
        scale_r = lane_stats[3, here, :]
        scale_hit = lane_stats[4, here, :]
        for t in range(tiles):
            cols = pl.ds(t * LANES, LANES)
            grad_ref[here, cols] = (
                ep_buf[here, cols] * scale_p
                - er_buf[here, cols] * scale_r
                + jnp.where(hits == t * LANES, scale_hit, 0.0)
            )
        return carry

    lax.fori_loop(0, chunks, grad_chunk, 0)

    others = all_seqs.at[pl.ds(0, n_dp - 1)]
    pltpu.make_async_copy(others, others, seq_recv).wait()
    table = all_seqs[...]
    place = length * seqs * lax.broadcasted_iota(jnp.int32, (n_dp, LANES), 0)
    place = place + lax.broadcasted_iota(jnp.int32, (n_dp, LANES), 1)
    found = [
        jnp.sum(jnp.where(place == ids[0, j] * length, table, 0.0), axis=0, keepdims=True)
        for j in range(seqs)
    ]
    partner_value = jnp.sum(jnp.concatenate(found, axis=0), axis=1, keepdims=True)
    margin = sign_col * (own_col - partner_value)
    slope_ref[...] = -jax.nn.sigmoid(-margin)
    loss_ref[...] = jnp.maximum(-margin, 0.0) + jnp.log1p(jnp.exp(-jnp.abs(margin)))

    sent = all_rows.at[pl.ds(0, n_tensor - 1)]
    pltpu.make_async_copy(sent, sent, row_send).wait()
    sent = all_seqs.at[pl.ds(0, n_dp - 1)]
    pltpu.make_async_copy(sent, sent, seq_send).wait()


def scale_kernel(grad_ref, slope_ref, out_hbm, out_buf, sems):
    rows, width = out_buf.shape
    seqs = slope_ref.shape[0]
    length = rows // seqs
    copies = []
    for j in range(seqs):
        here = pl.ds(j * length, length)
        out_buf[here, :] = grad_ref[here, :] * slope_ref[j : j + 1, 0:1]
        copy = pltpu.make_async_copy(out_buf.at[here], out_hbm.at[here], sems.at[j])
        copy.start()
        copies.append(copy)
    for copy in copies:
        copy.wait()


def shards(n_dp, n_tensor, policy_logits, reference_logits, targets, loss_mask, partner, chosen):
    rows, width = policy_logits.shape
    seqs = partner.shape[0]
    hbm = pl.BlockSpec(memory_space=pltpu.HBM)
    vmem = pl.BlockSpec(memory_space=pltpu.VMEM)
    grad, slope, loss = pl.pallas_call(
        functools.partial(stats_kernel, n_dp, n_tensor),
        out_shape=(
            pltpu.VMEM((rows, width), jnp.float32),
            pltpu.VMEM((seqs, LANES), jnp.float32),
            jax.ShapeDtypeStruct((seqs, LANES), jnp.float32),
        ),
        in_specs=[hbm] * 6,
        out_specs=(vmem, vmem, vmem),
        scratch_shapes=[
            pltpu.VMEM((rows, width), jnp.bfloat16),
            pltpu.VMEM((rows, width), jnp.bfloat16),
            pltpu.VMEM((rows, width), jnp.float32),
            pltpu.VMEM((rows, width), jnp.float32),
            pltpu.VMEM((2, rows), jnp.int32),
            pltpu.SMEM((2, seqs), jnp.int32),
            pltpu.VMEM((6, rows, LANES), jnp.float32),
            pltpu.VMEM((2, rows, LANES), jnp.int32),
            pltpu.VMEM((8, LANES), jnp.float32),
            pltpu.VMEM((n_tensor, 8, LANES), jnp.float32),
            pltpu.VMEM((1, LANES), jnp.float32),
            pltpu.VMEM((n_dp, LANES), jnp.float32),
            pltpu.SemaphoreType.DMA((2, rows // CHUNK)),
            pltpu.SemaphoreType.DMA((4,)),
            pltpu.SemaphoreType.DMA,
            pltpu.SemaphoreType.DMA,
            pltpu.SemaphoreType.DMA,
            pltpu.SemaphoreType.DMA,
        ],
        compiler_params=pltpu.CompilerParams(
            collective_id=0, has_side_effects=True, vmem_limit_bytes=32 * 1024 * 1024
        ),
        name="row_stats",
    )(policy_logits, reference_logits, targets, loss_mask, partner, chosen)
    logit_grad = pl.pallas_call(
        scale_kernel,
        out_shape=jax.ShapeDtypeStruct((rows, width), jnp.float32),
        in_specs=[vmem, vmem],
        out_specs=hbm,
        scratch_shapes=[
            pltpu.VMEM((rows, width), jnp.float32),
            pltpu.SemaphoreType.DMA((seqs,)),
        ],
        compiler_params=pltpu.CompilerParams(vmem_limit_bytes=32 * 1024 * 1024),
        name="scale_grad",
    )(grad, slope)
    return logit_grad, loss[:, 0]


def solution(mesh):
    return jax.shard_map(
        functools.partial(shards, mesh.shape["dp"], mesh.shape["tensor"]),
        mesh=mesh,
        in_specs=(P("dp", "tensor"), P("dp", "tensor"), P("dp"), P("dp"), P("dp"), P("dp")),
        out_specs=(P("dp", "tensor"), P("dp")),
        check_vma=False,
    )
```

time: 121 us -> 38.3 us (0.32)
  the two profiles are of different devices: /device:TPU:6 before, /device:TPU:1 now
where the time goes in v1:
time: 38.3 us; the launch traced here: 38.1 us
  Pallas kernels  31.6 us (83%)
  local copies, waits for them, and re-layouts  5.82 us (15%)
  between operations  0.66 us (2%)
    pallas_call x1, Pallas kernels, shards(): pl.pallas_call(functools.partial(stats_kernel, n_dp, n_tensor), out_shape...  30 us
    unnamed x12, local copies, waits for them, and re-layouts  5.2 us
    pallas_call x1, Pallas kernels, shards(): pl.pallas_call(scale_kernel, out_shape=jax.ShapeDtypeStruct((rows, width)...  1.56 us

profile of v1, /device:TPU:1, one launch (start us, length us, event | category | flops | bytes accessed | tf_op | source)
XLA Modules:
  0.0 38.1 jit_solution(14722483289438879819)
XLA Ops:
  0.6 0.0 copy-start
  0.6 1.3 %copy-done = bf16[128,4864]{1,0:T(8,128)(2,1)S(1)} copy-done((bf16[128,4864]{1,0:T(8,128)(2,1)S(1)}, bf16[128,4864]{1,0:T(8,128)(2,1)}, u32[]{:S(2)}) %copy-start) | copy-done | bytes 1245208
  1.9 0.0 copy-start.1
  1.9 1.3 %copy-done.1 = bf16[128,4864]{1,0:T(8,128)(2,1)S(1)} copy-done((bf16[128,4864]{1,0:T(8,128)(2,1)S(1)}, bf16[128,4864]{1,0:T(8,128)(2,1)}, u32[]{:S(2)}) %copy-start.1) | copy-done | bytes 1245208
  3.2 0.0 copy-start.2
  3.2 0.7 %copy-done.2 = s32[128]{0:T(128)S(1)} copy-done((s32[128]{0:T(128)S(1)}, s32[128]{0:T(128)}, u32[]{:S(2)}) %copy-start.2) | copy-done | bytes 536
  3.9 0.0 copy-start.3
  3.9 0.7 %copy-done.3 = s32[128]{0:T(128)S(1)} copy-done((s32[128]{0:T(128)S(1)}, s32[128]{0:T(128)}, u32[]{:S(2)}) %copy-start.3) | copy-done | bytes 536
  4.5 0.0 copy-start.4
  4.5 0.7 %copy-done.4 = s32[8]{0:T(128)S(1)} copy-done((s32[8]{0:T(128)S(1)}, s32[8]{0:T(128)}, u32[]{:S(2)}) %copy-start.4) | copy-done | bytes 56
  5.2 0.0 copy-start.5
  5.2 0.7 %copy-done.5 = s32[8]{0:T(128)S(1)} copy-done((s32[8]{0:T(128)S(1)}, s32[8]{0:T(128)}, u32[]{:S(2)}) %copy-start.5) | copy-done | bytes 56
  5.8 30.0 %row_stats.1 = (f32[128,4864]{1,0:T(8,128)S(1)}, f32[8,128]{1,0:T(8,128)S(1)}, f32[8,128]{1,0:T(8,128)S(1)}) custom-call(bf16[128,4864]{1,0:T(8,128)(2,1)S(1)} %copy-done, bf16[128,4864]{1,0:T(8,128)(2,1)S(1)} %copy-done.1, s32[128]{0:T(128)S(1)} %copy-done.2, s32[128]{0:T(128)S(1)} %copy-done.3, s32[8]{0:T(128)S(1)} %copy-done.4, s32[8]{0:T(128)S(1)} %copy-done.5), custom_call_target="tpu_custom_call" | custom-call | tf_op jit(solution)/shard_map/row_stats/pallas_call | solution.py:289
  35.9 1.6 %scale_grad.1 = f32[128,4864]{1,0:T(8,128)} custom-call(f32[128,4864]{1,0:T(8,128)S(1)} %get-tuple-element.5.grad_ref, f32[8,128]{1,0:T(8,128)S(1)} %get-tuple-element.6.slope_ref), custom_call_target="tpu_custom_call" | custom-call | tf_op jit(solution)/shard_map/scale_grad/pallas_call | solution.py:323
  37.4 0.6 %slice_reduce_fusion = f32[8]{0:T(128)} fusion(f32[8,128]{1,0:T(8,128)S(1)} %get-tuple-element.7), kind=kLoop, calls=%fused_computation | loop fusion | bytes 64 | tf_op jit(solution)/shard_map/slice | solution.py:335
Async XLA Ops:
  0.6 1.3 %copy-start = (bf16[128,4864]{1,0:T(8,128)(2,1)S(1)}, bf16[128,4864]{1,0:T(8,128)(2,1)}, u32[]{:S(2)}) copy-start(bf16[128,4864]{1,0:T(8,128)(2,1)} %p_hbm.1) | copy-start | bytes 3735556
  1.9 1.3 %copy-start.1 = (bf16[128,4864]{1,0:T(8,128)(2,1)S(1)}, bf16[128,4864]{1,0:T(8,128)(2,1)}, u32[]{:S(2)}) copy-start(bf16[128,4864]{1,0:T(8,128)(2,1)} %r_hbm.1) | copy-start | bytes 3735556
  3.2 0.7 %copy-start.2 = (s32[128]{0:T(128)S(1)}, s32[128]{0:T(128)}, u32[]{:S(2)}) copy-start(s32[128]{0:T(128)} %targets_hbm.1) | copy-start | bytes 1540
  3.9 0.7 %copy-start.3 = (s32[128]{0:T(128)S(1)}, s32[128]{0:T(128)}, u32[]{:S(2)}) copy-start(s32[128]{0:T(128)} %mask_hbm.1) | copy-start | bytes 1540
  4.5 0.7 %copy-start.4 = (s32[8]{0:T(128)S(1)}, s32[8]{0:T(128)}, u32[]{:S(2)}) copy-start(s32[8]{0:T(128)} %partner_hbm.1) | copy-start | bytes 100
  5.2 0.7 %copy-start.5 = (s32[8]{0:T(128)S(1)}, s32[8]{0:T(128)}, u32[]{:S(2)}) copy-start(s32[8]{0:T(128)} %chosen_hbm.1) | copy-start | bytes 100

commit v2 on v1

v2 whole, which is shorter than its diff:
```python
import functools
import jax
import jax.numpy as jnp
from jax import lax
from jax.experimental import pallas as pl
from jax.experimental.pallas import tpu as pltpu
from jax.sharding import PartitionSpec as P

beta_scale = 0.5
kl_scale = 0.25
MESH = pl.DeviceIdType.MESH
LANES = 128
CHUNK = 16
PARTS = 4


def ring(size):
    return sorted(range(1, size), key=lambda k: -min(k, size - k))


def stats_kernel(
    n_dp,
    n_tensor,
    n_z,
    p_hbm,
    r_hbm,
    targets_hbm,
    mask_hbm,
    partner_hbm,
    chosen_hbm,
    grad_ref,
    margin_ref,
    p_buf,
    r_buf,
    rows_int,
    ids,
    lane_stats,
    hit_set,
    own_rows,
    all_rows,
    own_seqs,
    all_seqs,
    chunk_sems,
    small_sems,
    row_send,
    row_recv,
    seq_send,
    seq_recv,
    known_sem,
):
    rows, width = p_buf.shape
    tiles = width // LANES
    chunks = rows // CHUNK
    seqs = partner_hbm.shape[0]
    length = rows // seqs
    n_x = n_dp // n_z
    my_dp = lax.axis_index("dp")
    my_tensor = lax.axis_index("tensor")
    my_x = my_dp // n_z
    my_z = lax.rem(my_dp, n_z)

    def tensor_peer(k):
        return {"tensor": lax.rem(my_tensor + k, n_tensor)}

    def dp_peer(x, z):
        return {"dp": lax.rem(my_x + x, n_x) * n_z + lax.rem(my_z + z, n_z)}

    barrier = pltpu.get_barrier_semaphore()
    greeted = [tensor_peer(k) for k in ring(n_tensor)]
    greeted += [dp_peer(0, z) for z in ring(n_z)]
    greeted += [dp_peer(x, 0) for x in ring(n_x)]
    for peer in greeted:
        pl.semaphore_signal(barrier, inc=1, device_id=peer, device_id_type=MESH)

    small = [
        pltpu.make_async_copy(targets_hbm, rows_int.at[0], small_sems.at[0]),
        pltpu.make_async_copy(mask_hbm, rows_int.at[1], small_sems.at[1]),
        pltpu.make_async_copy(partner_hbm, ids.at[0], small_sems.at[2]),
        pltpu.make_async_copy(chosen_hbm, ids.at[1], small_sems.at[3]),
    ]
    for copy in small:
        copy.start()

    def chunk_copies(c):
        here = pl.ds(pl.multiple_of(c * CHUNK, CHUNK), CHUNK)
        return (
            pltpu.make_async_copy(p_hbm.at[here], p_buf.at[here], chunk_sems.at[0, c]),
            pltpu.make_async_copy(r_hbm.at[here], r_buf.at[here], chunk_sems.at[1, c]),
        )

    for c in range(chunks):
        for copy in chunk_copies(c):
            copy.start()

    for copy in small:
        copy.wait()
    targets_row = rows_int[0:1, :] - my_tensor * width
    mask_row = rows_int[1:2, :].astype(jnp.float32)
    sub_r = lax.broadcasted_iota(jnp.int32, (LANES, LANES), 0)
    lane_r = lax.broadcasted_iota(jnp.int32, (LANES, LANES), 1)
    stacked = jnp.where(
        sub_r == 0, targets_row.astype(jnp.float32), jnp.where(sub_r == 1, mask_row, 0.0)
    )
    columns = stacked.T
    hit_set[...] = jnp.broadcast_to(columns[:, 0:1], (LANES, LANES)).astype(jnp.int32) - lane_r
    mask_col = columns[:, 1:2]

    def one_chunk(c, carry):
        for copy in chunk_copies(c):
            copy.wait()
        here = pl.ds(pl.multiple_of(c * CHUNK, CHUNK), CHUNK)
        top_p = p_buf[here, pl.ds(0, LANES)]
        top_r = r_buf[here, pl.ds(0, LANES)]
        for t in range(1, tiles):
            top_p = jnp.maximum(top_p, p_buf[here, pl.ds(t * LANES, LANES)])
            top_r = jnp.maximum(top_r, r_buf[here, pl.ds(t * LANES, LANES)])
        top_p = top_p.astype(jnp.float32)
        top_r = top_r.astype(jnp.float32)
        hits = hit_set[here, :]
        sum_p = jnp.zeros((CHUNK, LANES), jnp.float32)
        sum_r = sum_p
        cross = sum_p
        pick = sum_p
        for t in range(tiles):
            cols = pl.ds(t * LANES, LANES)
            p = p_buf[here, cols].astype(jnp.float32)
            r = r_buf[here, cols].astype(jnp.float32)
            e_p = jnp.exp(p - top_p)
            e_r = jnp.exp(r - top_r)
            gap = r - p
            sum_p += e_p
            sum_r += e_r
            cross += e_r * gap
            pick += jnp.where(hits == t * LANES, gap, 0.0)
        lane_stats[0, here, :] = top_p
        lane_stats[1, here, :] = top_r
        lane_stats[2, here, :] = sum_p
        lane_stats[3, here, :] = sum_r
        lane_stats[4, here, :] = cross
        lane_stats[5, here, :] = pick
        return carry

    lax.fori_loop(0, chunks, one_chunk, 0)

    top_p = lane_stats[0]
    top_r = lane_stats[1]
    peak_p = jnp.max(top_p, axis=1, keepdims=True)
    peak_r = jnp.max(top_r, axis=1, keepdims=True)
    scale_r = jnp.exp(top_r - peak_r)
    total_p = jnp.sum(lane_stats[2] * jnp.exp(top_p - peak_p), axis=1, keepdims=True)
    total_r = jnp.sum(lane_stats[3] * scale_r, axis=1, keepdims=True)
    cross = jnp.sum(lane_stats[4] * scale_r, axis=1, keepdims=True)
    pick = jnp.sum(lane_stats[5], axis=1, keepdims=True)
    part_p = peak_p + jnp.log(total_p)
    part_r = peak_r + jnp.log(total_r)
    packed = jnp.where(
        lane_r == 0,
        part_p,
        jnp.where(
            lane_r == 1,
            part_r,
            jnp.where(lane_r == 2, cross / total_r, jnp.where(lane_r == 3, pick, 0.0)),
        ),
    )
    own = packed.T[0:PARTS, :]
    own_rows[...] = own
    all_rows[my_tensor] = own

    pl.semaphore_wait(barrier, len(greeted))
    for k in ring(n_tensor):
        pltpu.make_async_remote_copy(
            src_ref=own_rows,
            dst_ref=all_rows.at[my_tensor],
            send_sem=row_send,
            recv_sem=row_recv,
            device_id=tensor_peer(k),
            device_id_type=MESH,
        ).start()

    for x in ring(n_x):
        pl.semaphore_signal(known_sem, inc=1, device_id=dp_peer(x, 0), device_id_type=MESH)

    sub_s = lax.broadcasted_iota(jnp.int32, (seqs, LANES), 0)
    lane_s = lax.broadcasted_iota(jnp.int32, (seqs, LANES), 1)
    place_col = jnp.zeros((seqs, LANES), jnp.int32)
    chosen_col = jnp.zeros((seqs, LANES), jnp.float32)
    for j in range(seqs):
        place_col = jnp.where(sub_s == j, lax.rem(ids[0, j], seqs) * length, place_col)
        chosen_col = jnp.where(sub_s == j, ids[1, j].astype(jnp.float32), chosen_col)
    sign_col = 2.0 * chosen_col - 1.0
    block_s = lane_s // length == sub_s

    pl.semaphore_wait(known_sem, n_x - 1)
    others = all_rows.at[pl.ds(0, n_tensor - 1)]
    pltpu.make_async_copy(others, others, row_recv).wait()
    parts = [all_rows[k] for k in range(n_tensor)]
    peak = functools.reduce(jnp.maximum, parts)
    weights = [jnp.exp(part - peak) for part in parts]
    total = functools.reduce(jnp.add, weights)
    norm = peak + jnp.log(total)
    cross_row = functools.reduce(
        jnp.add, [w[1:2, :] * part[2:3, :] for w, part in zip(weights, parts)]
    )
    pick_row = functools.reduce(jnp.add, parts)[3:4, :]
    norm_p = norm[0:1, :]
    norm_r = norm[1:2, :]
    kl_row = cross_row / total[1:2, :] - norm_r + norm_p
    ratio_row = norm_r - norm_p - pick_row
    value_row = mask_row * (beta_scale * ratio_row + kl_scale * kl_row)
    own_col = jnp.sum(jnp.where(block_s, value_row, 0.0), axis=1, keepdims=True)
    own = jnp.sum(jnp.where(block_s, own_col, 0.0), axis=0, keepdims=True)
    own_seqs[...] = own
    all_seqs[pl.ds(my_dp, 1), :] = own

    far = sorted(
        [(x, z) for x in range(n_x) for z in range(n_z) if x or z],
        key=lambda s: -min(s[0], n_x - s[0]) - min(s[1], n_z - s[1]),
    )
    for x, z in far:
        pltpu.make_async_remote_copy(
            src_ref=own_seqs,
            dst_ref=all_seqs.at[pl.ds(my_dp, 1)],
            send_sem=seq_send,
            recv_sem=seq_recv,
            device_id=dp_peer(x, z),
            device_id_type=MESH,
        ).start()

    stacked = jnp.where(sub_r == 0, norm_p, jnp.where(sub_r == 1, norm_r, 0.0))
    columns = stacked.T
    chosen_rows = jnp.concatenate(
        [jnp.broadcast_to(chosen_col[j : j + 1, :], (length, LANES)) for j in range(seqs)], axis=0
    )
    coef_hit = mask_col * (beta_scale * (2.0 * chosen_rows - 1.0))
    coef_kl = mask_col * (-kl_scale * (1.0 - chosen_rows))
    lane_stats[0] = jnp.broadcast_to(columns[:, 0:1], (LANES, LANES))
    lane_stats[1] = jnp.broadcast_to(columns[:, 1:2], (LANES, LANES))
    lane_stats[2] = coef_kl - coef_hit
    lane_stats[3] = coef_kl
    lane_stats[4] = coef_hit

    def grad_chunk(c, carry):
        here = pl.ds(pl.multiple_of(c * CHUNK, CHUNK), CHUNK)
        hits = hit_set[here, :]
        base_p = lane_stats[0, here, :]
        base_r = lane_stats[1, here, :]
        scale_p = lane_stats[2, here, :]
        scale_r = lane_stats[3, here, :]
        scale_hit = lane_stats[4, here, :]
        for t in range(tiles):
            cols = pl.ds(t * LANES, LANES)
            p = p_buf[here, cols].astype(jnp.float32)
            r = r_buf[here, cols].astype(jnp.float32)
            grad_ref[here, cols] = (
                jnp.exp(p - base_p) * scale_p
                - jnp.exp(r - base_r) * scale_r
                + jnp.where(hits == t * LANES, scale_hit, 0.0)
            )
        return carry

    lax.fori_loop(0, chunks, grad_chunk, 0)

    pltpu.make_async_copy(others, others, row_send).wait()
    others = all_seqs.at[pl.ds(0, n_dp - 1)]
    pltpu.make_async_copy(others, others, seq_send).wait()
    pltpu.make_async_copy(others, others, seq_recv).wait()
    partner_rows = jnp.zeros((seqs, LANES), jnp.float32)
    for j in range(seqs):
        row = all_seqs[pl.ds(ids[0, j] // seqs, 1), :]
        partner_rows = jnp.where(sub_s == j, row, partner_rows)
    partner_value = jnp.sum(
        jnp.where(lane_s == place_col, partner_rows, 0.0), axis=1, keepdims=True
    )
    margin_ref[...] = sign_col * (own_col - partner_value)


def scale_kernel(grad_ref, margin_ref, out_hbm, loss_hbm, out_buf, loss_buf, sems):
    rows, width = out_buf.shape
    seqs = margin_ref.shape[0]
    length = rows // seqs
    margin = margin_ref[...]
    slope = -jax.nn.sigmoid(-margin)
    copies = []
    for j in range(seqs):
        here = pl.ds(j * length, length)
        out_buf[here, :] = grad_ref[here, :] * slope[j : j + 1, 0:1]
        copy = pltpu.make_async_copy(out_buf.at[here], out_hbm.at[here], sems.at[j])
        copy.start()
        copies.append(copy)
    loss = jnp.maximum(-margin, 0.0) + jnp.log1p(jnp.exp(-jnp.abs(margin)))
    sub = lax.broadcasted_iota(jnp.int32, (seqs, LANES), 0)
    lane = lax.broadcasted_iota(jnp.int32, (seqs, LANES), 1)
    loss_buf[...] = jnp.sum(jnp.where(sub == lane, loss, 0.0), axis=0)[:seqs]
    copy = pltpu.make_async_copy(loss_buf, loss_hbm, sems.at[seqs])
    copy.start()
    copies.append(copy)
    for copy in copies:
        copy.wait()


def shards(n_dp, n_tensor, n_z, *arrays):
    rows, width = arrays[0].shape
    seqs = arrays[4].shape[0]
    hbm = pl.BlockSpec(memory_space=pltpu.HBM)
    vmem = pl.BlockSpec(memory_space=pltpu.VMEM)
    arrays = [pltpu.with_memory_space_constraint(array, pltpu.HBM) for array in arrays]
    grad, margin = pl.pallas_call(
        functools.partial(stats_kernel, n_dp, n_tensor, n_z),
        out_shape=(
            pltpu.VMEM((rows, width), jnp.float32),
            pltpu.VMEM((seqs, LANES), jnp.float32),
        ),
        in_specs=[hbm] * 6,
        out_specs=(vmem, vmem),
        scratch_shapes=[
            pltpu.VMEM((rows, width), jnp.bfloat16),
            pltpu.VMEM((rows, width), jnp.bfloat16),
            pltpu.VMEM((2, rows), jnp.int32),
            pltpu.SMEM((2, seqs), jnp.int32),
            pltpu.VMEM((6, rows, LANES), jnp.float32),
            pltpu.VMEM((rows, LANES), jnp.int32),
            pltpu.VMEM((PARTS, LANES), jnp.float32),
            pltpu.VMEM((n_tensor, PARTS, LANES), jnp.float32),
            pltpu.VMEM((1, LANES), jnp.float32),
            pltpu.VMEM((n_dp, LANES), jnp.float32),
            pltpu.SemaphoreType.DMA((2, rows // CHUNK)),
            pltpu.SemaphoreType.DMA((4,)),
            pltpu.SemaphoreType.DMA,
            pltpu.SemaphoreType.DMA,
            pltpu.SemaphoreType.DMA,
            pltpu.SemaphoreType.DMA,
            pltpu.SemaphoreType.REGULAR,
        ],
        compiler_params=pltpu.CompilerParams(
            collective_id=0, has_side_effects=True, vmem_limit_bytes=32 * 1024 * 1024
        ),
        name="row_stats",
    )(*arrays)
    return pl.pallas_call(
        scale_kernel,
        out_shape=(
            jax.ShapeDtypeStruct((rows, width), jnp.float32),
            jax.ShapeDtypeStruct((seqs,), jnp.float32),
        ),
        in_specs=[vmem, vmem],
        out_specs=(hbm, hbm),
        scratch_shapes=[
            pltpu.VMEM((rows, width), jnp.float32),
            pltpu.VMEM((seqs,), jnp.float32),
            pltpu.SemaphoreType.DMA((seqs + 1,)),
        ],
        compiler_params=pltpu.CompilerParams(vmem_limit_bytes=32 * 1024 * 1024),
        name="scale_grad",
    )(grad, margin)


def solution(mesh):
    n_dp, n_tensor = mesh.shape["dp"], mesh.shape["tensor"]
    n_z = 8 if n_dp % 8 == 0 and n_dp > 8 else n_dp // 2
    return jax.shard_map(
        functools.partial(shards, n_dp, n_tensor, n_z),
        mesh=mesh,
        in_specs=(P("dp", "tensor"), P("dp", "tensor"), P("dp"), P("dp"), P("dp"), P("dp")),
        out_specs=(P("dp", "tensor"), P("dp")),
        check_vma=False,
    )
```

time: 38.3 us -> 28.3 us (0.74)
  local copies, waits for them, and re-layouts: 5.82 us -> 0 us
  Pallas kernels: 31.6 us -> 27.5 us
    unnamed x12 -> x0, local copies, waits for them, and re-layouts: 5.2 us -> none
    pallas_call x2, Pallas kernels: 31.6 us -> 27.5 us  [the longest x1 25.9 us: shards(): pl.pallas_call(functools.partial(stats_kernel, n_dp, n_tensor, n_z), out_...]
    slice x1 -> x0, local copies, waits for them, and re-layouts: 0.63 us -> none  [shards(): return (logit_grad, loss[:, 0])]
where the time goes in v2:
time: 28.3 us; the launch traced here: 28.1 us
  Pallas kernels  27.5 us (97%)
  between operations  0.64 us (2%)
    pallas_call x1, Pallas kernels, shards(): pl.pallas_call(functools.partial(stats_kernel, n_dp, n_tensor, n_z), out_...  25.9 us
    pallas_call x1, Pallas kernels, shards(): pl.pallas_call(scale_kernel, out_shape=(jax.ShapeDtypeStruct((rows, width...  1.58 us

profile of v2, /device:TPU:1, one launch (start us, length us, event | category | flops | bytes accessed | tf_op | source)
XLA Modules:
  0.0 28.1 jit_solution(500000686611825812)
XLA Ops:
  0.6 25.9 %row_stats.1 = (f32[128,4864]{1,0:T(8,128)S(1)}, f32[8,128]{1,0:T(8,128)S(1)}) custom-call(bf16[128,4864]{1,0:T(8,128)(2,1)} %p_hbm.1, bf16[128,4864]{1,0:T(8,128)(2,1)} %r_hbm.1, s32[128]{0:T(128)} %targets_hbm.1, s32[128]{0:T(128)} %mask_hbm.1, s32[8]{0:T(128)} %partner_hbm.1, s32[8]{0:T(128)} %chosen_hbm.1), custom_call_target="tpu_custom_call" | custom-call | tf_op jit(solution)/shard_map/row_stats/pallas_call | solution.py:307
  26.6 1.6 %scale_grad.1 = (f32[128,4864]{1,0:T(8,128)}, f32[8]{0:T(128)}) custom-call(f32[128,4864]{1,0:T(8,128)S(1)} %get-tuple-element.4.grad_ref, f32[8,128]{1,0:T(8,128)S(1)} %get-tuple-element.5.margin_ref), custom_call_target="tpu_custom_call" | custom-call | tf_op jit(solution)/shard_map/scale_grad/pallas_call | solution.py:339

commit v3 on v2

--- a/solution.py
+++ b/solution.py
@@ -11,7 +11,10 @@
 MESH = pl.DeviceIdType.MESH
 LANES = 128
 CHUNK = 16
+GROUP = 32
+WAYS = 4
 PARTS = 4
+CORES = 2
 
 
 def ring(size):
@@ -40,13 +43,13 @@
     all_rows,
     own_seqs,
     all_seqs,
-    chunk_sems,
+    group_sems,
     small_sems,
     row_send,
     row_recv,
     seq_send,
     seq_recv,
-    known_sem,
+    known_sems,
 ):
     rows, width = p_buf.shape
     tiles = width // LANES
@@ -59,18 +62,23 @@
     my_x = my_dp // n_z
     my_z = lax.rem(my_dp, n_z)
 
+    my_y = my_tensor // CORES
+    my_core = lax.rem(my_tensor, CORES)
+    n_y = n_tensor // CORES
+    sibling = {"tensor": my_tensor + 1 - 2 * my_core}
+
+    def y_peer(y, core):
+        return {"tensor": lax.rem(my_y + y, n_y) * CORES + core}
+
     def tensor_peer(k):
         return {"tensor": lax.rem(my_tensor + k, n_tensor)}
 
     def dp_peer(x, z):
-        return {"dp": lax.rem(my_x + x, n_x) * n_z + lax.rem(my_z + z, n_z)}
-
-    barrier = pltpu.get_barrier_semaphore()
-    greeted = [tensor_peer(k) for k in ring(n_tensor)]
-    greeted += [dp_peer(0, z) for z in ring(n_z)]
-    greeted += [dp_peer(x, 0) for x in ring(n_x)]
-    for peer in greeted:
-        pl.semaphore_signal(barrier, inc=1, device_id=peer, device_id_type=MESH)
+        place = lax.rem(my_x + x, n_x) * n_z + lax.rem(my_z + z, n_z)
+        return {"dp": place, "tensor": my_y * CORES + 1}
+
+    def signal(sem, peer):
+        pl.semaphore_signal(sem, inc=1, device_id=peer, device_id_type=MESH)
 
     small = [
         pltpu.make_async_copy(targets_hbm, rows_int.at[0], small_sems.at[0]),
@@ -78,21 +86,33 @@
         pltpu.make_async_copy(partner_hbm, ids.at[0], small_sems.at[2]),
         pltpu.make_async_copy(chosen_hbm, ids.at[1], small_sems.at[3]),
     ]
-    for copy in small:
+    def group_copies(c):
+        here = pl.ds(pl.multiple_of(c * GROUP, GROUP), GROUP)
+        return (
+            pltpu.make_async_copy(p_hbm.at[here], p_buf.at[here], group_sems.at[0, c]),
+            pltpu.make_async_copy(r_hbm.at[here], r_buf.at[here], group_sems.at[1, c]),
+        )
+
+    for copy in small[:2]:
         copy.start()
-
-    def chunk_copies(c):
-        here = pl.ds(pl.multiple_of(c * CHUNK, CHUNK), CHUNK)
-        return (
-            pltpu.make_async_copy(p_hbm.at[here], p_buf.at[here], chunk_sems.at[0, c]),
-            pltpu.make_async_copy(r_hbm.at[here], r_buf.at[here], chunk_sems.at[1, c]),
-        )
-
-    for c in range(chunks):
-        for copy in chunk_copies(c):
+    for copy in group_copies(0):
+        copy.start()
+
+    barrier = pltpu.get_barrier_semaphore()
+    greeted = [(min(y, n_y - y), y_peer(y, 0)) for y in range(1, n_y)]
+    greeted += [(min(z, n_z - z), dp_peer(0, z)) for z in range(1, n_z)]
+    greeted += [(min(x, n_x - x), dp_peer(x, 0)) for x in range(1, n_x)]
+    for _, peer in sorted(greeted, key=lambda g: -g[0]):
+        signal(barrier, peer)
+    signal(barrier, sibling)
+
+    for c in range(1, rows // GROUP):
+        for copy in group_copies(c):
             copy.start()
-
-    for copy in small:
+    for copy in small[2:]:
+        copy.start()
+
+    for copy in small[:2]:
         copy.wait()
     targets_row = rows_int[0:1, :] - my_tensor * width
     mask_row = rows_int[1:2, :].astype(jnp.float32)
@@ -105,17 +125,25 @@
     hit_set[...] = jnp.broadcast_to(columns[:, 0:1], (LANES, LANES)).astype(jnp.int32) - lane_r
     mask_col = columns[:, 1:2]
 
-    def one_chunk(c, carry):
-        for copy in chunk_copies(c):
-            copy.wait()
-        here = pl.ds(pl.multiple_of(c * CHUNK, CHUNK), CHUNK)
-        top_p = p_buf[here, pl.ds(0, LANES)]
-        top_r = r_buf[here, pl.ds(0, LANES)]
-        for t in range(1, tiles):
-            top_p = jnp.maximum(top_p, p_buf[here, pl.ds(t * LANES, LANES)])
-            top_r = jnp.maximum(top_r, r_buf[here, pl.ds(t * LANES, LANES)])
-        top_p = top_p.astype(jnp.float32)
-        top_r = top_r.astype(jnp.float32)
+    diagonal = (
+        lax.broadcasted_iota(jnp.int32, (8, LANES), 1)
+        - lax.broadcasted_iota(jnp.int32, (8, LANES), 0)
+    )
+
+    def peak_of(buf, here):
+        tops = [buf[here, pl.ds(t * LANES, LANES)] for t in range(WAYS)]
+        for t in range(WAYS, tiles):
+            tops[t % WAYS] = jnp.maximum(tops[t % WAYS], buf[here, pl.ds(t * LANES, LANES)])
+        return functools.reduce(jnp.maximum, tops).astype(jnp.float32)
+
+    def sums_of(start):
+        here = pl.ds(pl.multiple_of(start, CHUNK), CHUNK)
+        top_p = peak_of(p_buf, here)
+        top_r = peak_of(r_buf, here)
+        peak_p = jnp.max(top_p, axis=1, keepdims=True)
+        peak_r = jnp.max(top_r, axis=1, keepdims=True)
+        scale_p = jnp.exp(top_p - peak_p)
+        scale_r = jnp.exp(top_r - peak_r)
         hits = hit_set[here, :]
         sum_p = jnp.zeros((CHUNK, LANES), jnp.float32)
         sum_r = sum_p
@@ -131,42 +159,54 @@
             sum_p += e_p
             sum_r += e_r
             cross += e_r * gap
-            pick += jnp.where(hits == t * LANES, gap, 0.0)
-        lane_stats[0, here, :] = top_p
-        lane_stats[1, here, :] = top_r
-        lane_stats[2, here, :] = sum_p
-        lane_stats[3, here, :] = sum_r
-        lane_stats[4, here, :] = cross
-        lane_stats[5, here, :] = pick
-        return carry
-
-    lax.fori_loop(0, chunks, one_chunk, 0)
-
-    top_p = lane_stats[0]
-    top_r = lane_stats[1]
-    peak_p = jnp.max(top_p, axis=1, keepdims=True)
-    peak_r = jnp.max(top_r, axis=1, keepdims=True)
-    scale_r = jnp.exp(top_r - peak_r)
-    total_p = jnp.sum(lane_stats[2] * jnp.exp(top_p - peak_p), axis=1, keepdims=True)
-    total_r = jnp.sum(lane_stats[3] * scale_r, axis=1, keepdims=True)
-    cross = jnp.sum(lane_stats[4] * scale_r, axis=1, keepdims=True)
-    pick = jnp.sum(lane_stats[5], axis=1, keepdims=True)
-    part_p = peak_p + jnp.log(total_p)
-    part_r = peak_r + jnp.log(total_r)
-    packed = jnp.where(
-        lane_r == 0,
-        part_p,
-        jnp.where(
-            lane_r == 1,
-            part_r,
-            jnp.where(lane_r == 2, cross / total_r, jnp.where(lane_r == 3, pick, 0.0)),
-        ),
-    )
-    own = packed.T[0:PARTS, :]
-    own_rows[...] = own
-    all_rows[my_tensor] = own
-
-    pl.semaphore_wait(barrier, len(greeted))
+            pick = jnp.where(hits == t * LANES, gap, pick)
+        return sum_p * scale_p, sum_r * scale_r, cross * scale_r, pick, peak_p, peak_r
+
+    def add_rows(acc, start, sums):
+        total_p, total_r, cross, pick = [
+            jnp.sum(part, axis=1, keepdims=True) for part in sums[:4]
+        ]
+        part_p = sums[4] + jnp.log(total_p)
+        part_r = sums[5] + jnp.log(total_r)
+        columns = (part_p, part_r, cross / total_r, pick)
+        out = []
+        for total, column in zip(acc, columns):
+            for g in range(0, CHUNK, 8):
+                total = total + jnp.where(diagonal == start + g, column[g : g + 8, :], 0.0)
+            out.append(total)
+        return tuple(out)
+
+    def one_group(c, carry):
+        acc, before = carry
+        for copy in group_copies(c):
+            copy.wait()
+        for g in range(0, GROUP, CHUNK):
+            start = c * GROUP + g
+            sums = sums_of(start)
+            acc = add_rows(acc, start - CHUNK, before)
+            before = sums
+        return acc, before
+
+    ones = jnp.ones((CHUNK, LANES), jnp.float32)
+    column = jnp.zeros((CHUNK, 1), jnp.float32)
+    zero = jnp.zeros((8, LANES), jnp.float32)
+    start = ((zero,) * PARTS, (ones, ones, ones, ones, column, column))
+    acc, sums = lax.fori_loop(0, rows // GROUP, one_group, start)
+    acc = add_rows(acc, rows - CHUNK, sums)
+
+    for k in range(PARTS):
+        own_rows[k : k + 1, :] = jnp.sum(acc[k], axis=0, keepdims=True)
+    all_rows[my_tensor] = own_rows[...]
+
+    @pl.when(my_core == 0)
+    def _():
+        pl.semaphore_wait(barrier, 2 * n_y - 1)
+        signal(known_sems.at[0], sibling)
+
+    @pl.when(my_core == 1)
+    def _():
+        pl.semaphore_wait(known_sems.at[0], 1)
+
     for k in ring(n_tensor):
         pltpu.make_async_remote_copy(
             src_ref=own_rows,
@@ -177,8 +217,20 @@
             device_id_type=MESH,
         ).start()
 
-    for x in ring(n_x):
-        pl.semaphore_signal(known_sem, inc=1, device_id=dp_peer(x, 0), device_id_type=MESH)
+    @pl.when(my_core == 1)
+    def _():
+        pl.semaphore_wait(barrier, 2 * (n_z + n_x) - 3)
+        for x in ring(n_x):
+            signal(known_sems.at[1], dp_peer(x, 0))
+        pl.semaphore_wait(known_sems.at[1], n_x - 1)
+        signal(known_sems.at[2], sibling)
+
+    @pl.when(my_core == 0)
+    def _():
+        pl.semaphore_wait(known_sems.at[2], 1)
+
+    for copy in small[2:]:
+        copy.wait()
 
     sub_s = lax.broadcasted_iota(jnp.int32, (seqs, LANES), 0)
     lane_s = lax.broadcasted_iota(jnp.int32, (seqs, LANES), 1)
@@ -190,7 +242,6 @@
     sign_col = 2.0 * chosen_col - 1.0
     block_s = lane_s // length == sub_s
 
-    pl.semaphore_wait(known_sem, n_x - 1)
     others = all_rows.at[pl.ds(0, n_tensor - 1)]
     pltpu.make_async_copy(others, others, row_recv).wait()
     parts = [all_rows[k] for k in range(n_tensor)]
@@ -212,17 +263,15 @@
     own_seqs[...] = own
     all_seqs[pl.ds(my_dp, 1), :] = own
 
-    far = sorted(
-        [(x, z) for x in range(n_x) for z in range(n_z) if x or z],
-        key=lambda s: -min(s[0], n_x - s[0]) - min(s[1], n_z - s[1]),
-    )
-    for x, z in far:
+    my_rank = my_z * n_x + my_x
+    for k in range(n_dp - 1):
+        rank = k + (k + n_dp - my_rank) // n_dp
         pltpu.make_async_remote_copy(
             src_ref=own_seqs,
             dst_ref=all_seqs.at[pl.ds(my_dp, 1)],
             send_sem=seq_send,
             recv_sem=seq_recv,
-            device_id=dp_peer(x, z),
+            device_id={"dp": lax.rem(rank, n_x) * n_z + rank // n_x},
             device_id_type=MESH,
         ).start()
 
@@ -317,19 +366,19 @@
             pltpu.VMEM((rows, width), jnp.bfloat16),
             pltpu.VMEM((2, rows), jnp.int32),
             pltpu.SMEM((2, seqs), jnp.int32),
-            pltpu.VMEM((6, rows, LANES), jnp.float32),
+            pltpu.VMEM((5, rows, LANES), jnp.float32),
             pltpu.VMEM((rows, LANES), jnp.int32),
             pltpu.VMEM((PARTS, LANES), jnp.float32),
             pltpu.VMEM((n_tensor, PARTS, LANES), jnp.float32),
             pltpu.VMEM((1, LANES), jnp.float32),
             pltpu.VMEM((n_dp, LANES), jnp.float32),
-            pltpu.SemaphoreType.DMA((2, rows // CHUNK)),
+            pltpu.SemaphoreType.DMA((2, rows // GROUP)),
             pltpu.SemaphoreType.DMA((4,)),
             pltpu.SemaphoreType.DMA,
             pltpu.SemaphoreType.DMA,
             pltpu.SemaphoreType.DMA,
             pltpu.SemaphoreType.DMA,
-            pltpu.SemaphoreType.REGULAR,
+            pltpu.SemaphoreType.REGULAR((3,)),
         ],
         compiler_params=pltpu.CompilerParams(
             collective_id=0, has_side_effects=True, vmem_limit_bytes=32 * 1024 * 1024

time: 28.3 us -> 27 us (0.954)
  Pallas kernels: 27.5 us -> 26.2 us
    pallas_call x1, Pallas kernels: 25.9 us -> 24.6 us  [shards(): pl.pallas_call(functools.partial(stats_kernel, n_dp, n_tensor, n_z), out_...]
where the time goes in v3:
time: 27 us; the launch traced here: 26.8 us
  Pallas kernels  26.2 us (97%)
  between operations  0.64 us (2%)
    pallas_call x1, Pallas kernels, shards(): pl.pallas_call(functools.partial(stats_kernel, n_dp, n_tensor, n_z), out_...  24.6 us
    pallas_call x1, Pallas kernels, shards(): pl.pallas_call(scale_kernel, out_shape=(jax.ShapeDtypeStruct((rows, width...  1.58 us

profile of v3, /device:TPU:1, one launch (start us, length us, event | category | flops | bytes accessed | tf_op | source)
XLA Modules:
  0.0 26.8 jit_solution(7484995506935817720)
XLA Ops:
  0.6 24.6 %row_stats.1 = (f32[128,4864]{1,0:T(8,128)S(1)}, f32[8,128]{1,0:T(8,128)S(1)}) custom-call(bf16[128,4864]{1,0:T(8,128)(2,1)} %p_hbm.1, bf16[128,4864]{1,0:T(8,128)(2,1)} %r_hbm.1, s32[128]{0:T(128)} %targets_hbm.1, s32[128]{0:T(128)} %mask_hbm.1, s32[8]{0:T(128)} %partner_hbm.1, s32[8]{0:T(128)} %chosen_hbm.1), custom_call_target="tpu_custom_call" | custom-call | tf_op jit(solution)/shard_map/row_stats/pallas_call | solution.py:356
  25.3 1.6 %scale_grad.1 = (f32[128,4864]{1,0:T(8,128)}, f32[8]{0:T(128)}) custom-call(f32[128,4864]{1,0:T(8,128)S(1)} %get-tuple-element.4.grad_ref, f32[8,128]{1,0:T(8,128)S(1)} %get-tuple-element.5.margin_ref), custom_call_target="tpu_custom_call" | custom-call | tf_op jit(solution)/shard_map/scale_grad/pallas_call | solution.py:388

commit v4 on v3

--- a/solution.py
+++ b/solution.py
@@ -70,9 +70,6 @@
     def y_peer(y, core):
         return {"tensor": lax.rem(my_y + y, n_y) * CORES + core}
 
-    def tensor_peer(k):
-        return {"tensor": lax.rem(my_tensor + k, n_tensor)}
-
     def dp_peer(x, z):
         place = lax.rem(my_x + x, n_x) * n_z + lax.rem(my_z + z, n_z)
         return {"dp": place, "tensor": my_y * CORES + 1}
@@ -93,42 +90,42 @@
             pltpu.make_async_copy(r_hbm.at[here], r_buf.at[here], group_sems.at[1, c]),
         )
 
-    for copy in small[:2]:
+    barrier = pltpu.get_barrier_semaphore()
+
+    def greet_y():
+        signal(barrier, sibling)
+        for y in ring(n_y):
+            signal(barrier, y_peer(y, 0))
+
+    def greet_dp():
+        for z in ring(n_z):
+            signal(barrier, dp_peer(0, z))
+        for x in ring(n_x):
+            signal(barrier, dp_peer(x, 0))
+
+    def read(*groups):
+        for c in groups:
+            for copy in group_copies(c):
+                copy.start()
+
+    read(0)
+    small[0].start()
+    greet_dp()
+    read(1, 2, 3)
+    greet_y()
+    for copy in small[1:]:
         copy.start()
-    for copy in group_copies(0):
-        copy.start()
-
-    barrier = pltpu.get_barrier_semaphore()
-    greeted = [(min(y, n_y - y), y_peer(y, 0)) for y in range(1, n_y)]
-    greeted += [(min(z, n_z - z), dp_peer(0, z)) for z in range(1, n_z)]
-    greeted += [(min(x, n_x - x), dp_peer(x, 0)) for x in range(1, n_x)]
-    for _, peer in sorted(greeted, key=lambda g: -g[0]):
-        signal(barrier, peer)
-    signal(barrier, sibling)
-
-    for c in range(1, rows // GROUP):
-        for copy in group_copies(c):
-            copy.start()
-    for copy in small[2:]:
-        copy.start()
-
-    for copy in small[:2]:
-        copy.wait()
-    targets_row = rows_int[0:1, :] - my_tensor * width
-    mask_row = rows_int[1:2, :].astype(jnp.float32)
-    sub_r = lax.broadcasted_iota(jnp.int32, (LANES, LANES), 0)
-    lane_r = lax.broadcasted_iota(jnp.int32, (LANES, LANES), 1)
-    stacked = jnp.where(
-        sub_r == 0, targets_row.astype(jnp.float32), jnp.where(sub_r == 1, mask_row, 0.0)
-    )
-    columns = stacked.T
-    hit_set[...] = jnp.broadcast_to(columns[:, 0:1], (LANES, LANES)).astype(jnp.int32) - lane_r
-    mask_col = columns[:, 1:2]
+
+    small[0].wait()
+    targets_row = (rows_int[0:1, :] - my_tensor * width).astype(jnp.float32)
 
     diagonal = (
         lax.broadcasted_iota(jnp.int32, (8, LANES), 1)
         - lax.broadcasted_iota(jnp.int32, (8, LANES), 0)
     )
+
+    sub_c = lax.broadcasted_iota(jnp.int32, (CHUNK, LANES), 0)
+    lane_c = lax.broadcasted_iota(jnp.int32, (CHUNK, LANES), 1)
 
     def peak_of(buf, here):
         tops = [buf[here, pl.ds(t * LANES, LANES)] for t in range(WAYS)]
@@ -144,7 +141,9 @@
         peak_r = jnp.max(top_r, axis=1, keepdims=True)
         scale_p = jnp.exp(top_p - peak_p)
         scale_r = jnp.exp(top_r - peak_r)
-        hits = hit_set[here, :]
+        own_target = jnp.where(lane_c == sub_c + start, targets_row, 0.0)
+        hits = jnp.sum(own_target, axis=1, keepdims=True).astype(jnp.int32) - lane_c
+        hit_set[here, :] = hits
         sum_p = jnp.zeros((CHUNK, LANES), jnp.float32)
         sum_r = sum_p
         cross = sum_p
@@ -201,21 +200,33 @@
     @pl.when(my_core == 0)
     def _():
         pl.semaphore_wait(barrier, 2 * n_y - 1)
-        signal(known_sems.at[0], sibling)
 
     @pl.when(my_core == 1)
     def _():
         pl.semaphore_wait(known_sems.at[0], 1)
 
-    for k in ring(n_tensor):
+    def send_rows(peer):
         pltpu.make_async_remote_copy(
             src_ref=own_rows,
             dst_ref=all_rows.at[my_tensor],
             send_sem=row_send,
             recv_sem=row_recv,
-            device_id=tensor_peer(k),
+            device_id=peer,
             device_id_type=MESH,
         ).start()
+
+    far_y, *near_y = ring(n_y)
+    send_rows(y_peer(far_y, 1))
+    send_rows(y_peer(far_y, 0))
+
+    @pl.when(my_core == 0)
+    def _():
+        signal(known_sems.at[0], sibling)
+
+    for y in near_y:
+        send_rows(y_peer(y, 1))
+        send_rows(y_peer(y, 0))
+    send_rows(sibling)
 
     @pl.when(my_core == 1)
     def _():
@@ -229,8 +240,11 @@
     def _():
         pl.semaphore_wait(known_sems.at[2], 1)
 
-    for copy in small[2:]:
+    for copy in small[1:]:
         copy.wait()
+    mask_row = rows_int[1:2, :].astype(jnp.float32)
+    sub_r = lax.broadcasted_iota(jnp.int32, (LANES, LANES), 0)
+    mask_col = jnp.where(sub_r == 0, mask_row, 0.0).T[:, 0:1]
 
     sub_s = lax.broadcasted_iota(jnp.int32, (seqs, LANES), 0)
     lane_s = lax.broadcasted_iota(jnp.int32, (seqs, LANES), 1)

time: 27 us -> 26.8 us (level)
  no operation moved by 1% of the time
where the time goes in v4:
time: 26.8 us; the launch traced here: 26.7 us
  Pallas kernels  26 us (97%)
  between operations  0.64 us (2%)
    pallas_call x1, Pallas kernels, shards(): pl.pallas_call(functools.partial(stats_kernel, n_dp, n_tensor, n_z), out_...  24.5 us
    pallas_call x1, Pallas kernels, shards(): pl.pallas_call(scale_kernel, out_shape=(jax.ShapeDtypeStruct((rows, width...  1.58 us

profile of v4, /device:TPU:1, one launch (start us, length us, event | category | flops | bytes accessed | tf_op | source)
XLA Modules:
  0.0 26.7 jit_solution(17524142574123634885)
XLA Ops:
  0.6 24.5 %row_stats.1 = (f32[128,4864]{1,0:T(8,128)S(1)}, f32[8,128]{1,0:T(8,128)S(1)}) custom-call(bf16[128,4864]{1,0:T(8,128)(2,1)} %p_hbm.1, bf16[128,4864]{1,0:T(8,128)(2,1)} %r_hbm.1, s32[128]{0:T(128)} %targets_hbm.1, s32[128]{0:T(128)} %mask_hbm.1, s32[8]{0:T(128)} %partner_hbm.1, s32[8]{0:T(128)} %chosen_hbm.1), custom_call_target="tpu_custom_call" | custom-call | tf_op jit(solution)/shard_map/row_stats/pallas_call | solution.py:370
  25.1 1.6 %scale_grad.1 = (f32[128,4864]{1,0:T(8,128)}, f32[8]{0:T(128)}) custom-call(f32[128,4864]{1,0:T(8,128)S(1)} %get-tuple-element.4.grad_ref, f32[8,128]{1,0:T(8,128)S(1)} %get-tuple-element.5.margin_ref), custom_call_target="tpu_custom_call" | custom-call | tf_op jit(solution)/shard_map/scale_grad/pallas_call | solution.py:402

commit v5 on v4

--- a/solution.py
+++ b/solution.py
@@ -10,7 +10,7 @@
 kl_scale = 0.25
 MESH = pl.DeviceIdType.MESH
 LANES = 128
-CHUNK = 16
+CHUNK = 32
 GROUP = 32
 WAYS = 4
 PARTS = 4
@@ -19,6 +19,12 @@
 
 def ring(size):
     return sorted(range(1, size), key=lambda k: -min(k, size - k))
+
+
+def tree(combine, items):
+    while len(items) > 1:
+        items = [combine(*items[k : k + 2]) if k + 1 < len(items) else items[k] for k in range(0, len(items), 2)]
+    return items[0]
 
 
 def stats_kernel(
@@ -113,8 +119,6 @@
     greet_dp()
     read(1, 2, 3)
     greet_y()
-    for copy in small[1:]:
-        copy.start()
 
     small[0].wait()
     targets_row = (rows_int[0:1, :] - my_tensor * width).astype(jnp.float32)
@@ -228,6 +232,9 @@
         send_rows(y_peer(y, 0))
     send_rows(sibling)
 
+    for copy in small[1:]:
+        copy.start()
+
     @pl.when(my_core == 1)
     def _():
         pl.semaphore_wait(barrier, 2 * (n_z + n_x) - 3)
@@ -259,14 +266,14 @@
     others = all_rows.at[pl.ds(0, n_tensor - 1)]
     pltpu.make_async_copy(others, others, row_recv).wait()
     parts = [all_rows[k] for k in range(n_tensor)]
-    peak = functools.reduce(jnp.maximum, parts)
+    peak = tree(jnp.maximum, parts)
     weights = [jnp.exp(part - peak) for part in parts]
-    total = functools.reduce(jnp.add, weights)
+    total = tree(jnp.add, weights)
     norm = peak + jnp.log(total)
-    cross_row = functools.reduce(
+    cross_row = tree(
         jnp.add, [w[1:2, :] * part[2:3, :] for w, part in zip(weights, parts)]
     )
-    pick_row = functools.reduce(jnp.add, parts)[3:4, :]
+    pick_row = tree(jnp.add, parts)[3:4, :]
     norm_p = norm[0:1, :]
     norm_r = norm[1:2, :]
     kl_row = cross_row / total[1:2, :] - norm_r + norm_p
@@ -323,10 +330,8 @@
 
     lax.fori_loop(0, chunks, grad_chunk, 0)
 
-    pltpu.make_async_copy(others, others, row_send).wait()
-    others = all_seqs.at[pl.ds(0, n_dp - 1)]
-    pltpu.make_async_copy(others, others, seq_send).wait()
-    pltpu.make_async_copy(others, others, seq_recv).wait()
+    others_dp = all_seqs.at[pl.ds(0, n_dp - 1)]
+    pltpu.make_async_copy(others_dp, others_dp, seq_recv).wait()
     partner_rows = jnp.zeros((seqs, LANES), jnp.float32)
     for j in range(seqs):
         row = all_seqs[pl.ds(ids[0, j] // seqs, 1), :]
@@ -335,6 +340,8 @@
         jnp.where(lane_s == place_col, partner_rows, 0.0), axis=1, keepdims=True
     )
     margin_ref[...] = sign_col * (own_col - partner_value)
+    pltpu.make_async_copy(others, others, row_send).wait()
+    pltpu.make_async_copy(others_dp, others_dp, seq_send).wait()
 
 
 def scale_kernel(grad_ref, margin_ref, out_hbm, loss_hbm, out_buf, loss_buf, sems):

time: 26.8 us -> 26.8 us (level)
  no operation moved by 1% of the time
where the time goes in v5:
time: 26.8 us; the launch traced here: 26.6 us
  Pallas kernels  26 us (97%)
  between operations  0.64 us (2%)
    pallas_call x1, Pallas kernels, shards(): pl.pallas_call(functools.partial(stats_kernel, n_dp, n_tensor, n_z), out_...  24.4 us
    pallas_call x1, Pallas kernels, shards(): pl.pallas_call(scale_kernel, out_shape=(jax.ShapeDtypeStruct((rows, width...  1.58 us

profile of v5, /device:TPU:1, one launch (start us, length us, event | category | flops | bytes accessed | tf_op | source)
XLA Modules:
  0.0 26.6 jit_solution(9433939820541339522)
XLA Ops:
  0.6 24.4 %row_stats.1 = (f32[128,4864]{1,0:T(8,128)S(1)}, f32[8,128]{1,0:T(8,128)S(1)}) custom-call(bf16[128,4864]{1,0:T(8,128)(2,1)} %p_hbm.1, bf16[128,4864]{1,0:T(8,128)(2,1)} %r_hbm.1, s32[128]{0:T(128)} %targets_hbm.1, s32[128]{0:T(128)} %mask_hbm.1, s32[8]{0:T(128)} %partner_hbm.1, s32[8]{0:T(128)} %chosen_hbm.1), custom_call_target="tpu_custom_call" | custom-call | tf_op jit(solution)/shard_map/row_stats/pallas_call | solution.py:377
  25.1 1.6 %scale_grad.1 = (f32[128,4864]{1,0:T(8,128)}, f32[8]{0:T(128)}) custom-call(f32[128,4864]{1,0:T(8,128)S(1)} %get-tuple-element.4.grad_ref, f32[8,128]{1,0:T(8,128)S(1)} %get-tuple-element.5.margin_ref), custom_call_target="tpu_custom_call" | custom-call | tf_op jit(solution)/shard_map/scale_grad/pallas_call | solution.py:409

commit v6 on v5

--- a/solution.py
+++ b/solution.py
@@ -114,10 +114,9 @@
             for copy in group_copies(c):
                 copy.start()
 
-    read(0)
     small[0].start()
+    read(0, 1, 2, 3)
     greet_dp()
-    read(1, 2, 3)
     greet_y()
 
     small[0].wait()
@@ -194,7 +193,9 @@
     column = jnp.zeros((CHUNK, 1), jnp.float32)
     zero = jnp.zeros((8, LANES), jnp.float32)
     start = ((zero,) * PARTS, (ones, ones, ones, ones, column, column))
-    acc, sums = lax.fori_loop(0, rows // GROUP, one_group, start)
+    acc, sums = start
+    for c in range(rows // GROUP):
+        acc, sums = one_group(c, (acc, sums))
     acc = add_rows(acc, rows - CHUNK, sums)
 
     for k in range(PARTS):

time: 26.8 us -> 27 us (level)
  no operation moved by 1% of the time
where the time goes in v6:
time: 27 us; the launch traced here: 26.9 us
  Pallas kernels  26.2 us (97%)
  between operations  0.64 us (2%)
    pallas_call x1, Pallas kernels, shards(): pl.pallas_call(functools.partial(stats_kernel, n_dp, n_tensor, n_z), out_...  24.7 us
    pallas_call x1, Pallas kernels, shards(): pl.pallas_call(scale_kernel, out_shape=(jax.ShapeDtypeStruct((rows, width...  1.58 us

profile of v6, /device:TPU:1, one launch (start us, length us, event | category | flops | bytes accessed | tf_op | source)
XLA Modules:
  0.0 26.9 jit_solution(14251585295204121257)
XLA Ops:
  0.6 24.7 %row_stats.1 = (f32[128,4864]{1,0:T(8,128)S(1)}, f32[8,128]{1,0:T(8,128)S(1)}) custom-call(bf16[128,4864]{1,0:T(8,128)(2,1)} %p_hbm.1, bf16[128,4864]{1,0:T(8,128)(2,1)} %r_hbm.1, s32[128]{0:T(128)} %targets_hbm.1, s32[128]{0:T(128)} %mask_hbm.1, s32[8]{0:T(128)} %partner_hbm.1, s32[8]{0:T(128)} %chosen_hbm.1), custom_call_target="tpu_custom_call" | custom-call | tf_op jit(solution)/shard_map/row_stats/pallas_call | solution.py:378
  25.3 1.6 %scale_grad.1 = (f32[128,4864]{1,0:T(8,128)}, f32[8]{0:T(128)}) custom-call(f32[128,4864]{1,0:T(8,128)S(1)} %get-tuple-element.4.grad_ref, f32[8,128]{1,0:T(8,128)S(1)} %get-tuple-element.5.margin_ref), custom_call_target="tpu_custom_call" | custom-call | tf_op jit(solution)/shard_map/scale_grad/pallas_call | solution.py:410
